TPU v7x, 32 devices: a whole 2x2x4 slice. The times are simulated.
32 devices in a mesh: row: 4 (over x, core), col: 8 (over z, y).
Axes of the slice: x: 2, y: 2, z: 4, core: 2. Of those that a mesh axis runs over, the one named last changes fastest.
Arguments:
- frames: bfloat16 [1536, 4096], P('row', 'col'), may hold values from -6 to 6
- gain: float32 [4096], replicated, may hold values from 0.3 to 10
- w_value: bfloat16 [4096, 4096], P('row', 'col'), may hold values from -0.09375 to 0.09375
- w_gate: bfloat16 [4096, 4096], P('row', 'col'), may hold values from -0.09375 to 0.09375
- kernel: float32 [31, 4096], P(None, 'col'), may hold values from -1.5 to 1.5
- bias: float32 [4096], P('col'), may hold values from -3 to 3
- w_out: bfloat16 [4096, 4096], P('row', 'col'), may hold values from -0.09375 to 0.09375
- grad_out: bfloat16 [1536, 4096], P('row', 'col'), may hold values from -6 to 6
Outputs:
- encoded: bfloat16 [1536, 4096], P('row', 'col')
- input_grad: bfloat16 [1536, 4096], P('row', 'col')
- grad_value: float32 [4096, 4096], P('row', 'col')
- grad_gate: float32 [4096, 4096], P('row', 'col')
- grad_kernel: float32 [31, 4096], P(None, 'col')
- grad_bias: float32 [4096], P('col')
- grad_out_weight: float32 [4096, 4096], P('row', 'col')
- grad_gain: float32 [4096], P('col')
All inputs are finite; a program needn't handle non-finite values.
Results may differ from a plain program's by a relative error of at most 0.035.
Values may be sent and summed in bfloat16 or wider, within the bound.
A program may use at most 128 MiB of HBM per device.

v0:
```python
import jax
import jax.numpy as jnp
from jax import lax
from jax.experimental import pallas as pl
from jax.experimental.pallas import tpu as pltpu
from jax.sharding import PartitionSpec as P

K = 31
LEN = 2048
HALF = K // 2
epsilon = 1e-05
MESH = pl.DeviceIdType.MESH
ANY = pl.BlockSpec(memory_space=pl.ANY)
VMEM = pl.BlockSpec(memory_space=pltpu.VMEM)
DMA = pltpu.SemaphoreType.DMA


def send(src, dst, sent, arrived, row, col):
    return pltpu.make_async_remote_copy(
        src_ref=src,
        dst_ref=dst,
        send_sem=sent,
        recv_sem=arrived,
        device_id=(row, col),
        device_id_type=MESH,
    )


def await_bytes(ref, sem):
    pltpu.make_async_copy(ref, ref, sem).wait()


def span(index, size):
    if isinstance(index, int):
        return pl.ds(index * size, size)
    return pl.ds(pl.multiple_of(index * size, size), size)


def by_rows(rows, cols, body):
    chunk = max(16, min(rows, 16384 // cols))
    while rows % chunk:
        chunk -= 16

    @pl.loop(0, rows // chunk)
    def _(step):
        body(span(step, chunk))


class Spread:
    def __init__(self, n, m, block, by_frames, cuts):
        self.n, self.m, self.block, self.by_frames, self.cuts = n, m, block, by_frames, cuts
        a, b = block
        whole = (n * a, m * b) if by_frames else (a, n * m * b)
        self.out_shape = [jax.ShapeDtypeStruct(whole, jnp.bfloat16)]
        self.out_specs = [VMEM]
        self.in_specs = [ANY]
        self.scratch = [DMA((n, cuts, m)), DMA((2 + m, n * cuts)), DMA((cuts,))]
        self.phases = n * cuts + 2

    def part(self, ref, k, y, cut):
        a, b = self.block
        high = a // self.cuts
        if self.by_frames:
            return ref.at[span(k * self.cuts + cut, high), span(y, b)]
        return ref.at[span(cut, high), span(y * self.n + k, b)]

    def run(self, phase, refs):
        x, out, arrived, sent, first = refs
        n, m, cuts = self.n, self.m, self.cuts
        r, c = lax.axis_index("row"), lax.axis_index("col")
        z, y = c // m, c % m

        def moves(q):
            k, cut = q // cuts, q % cuts
            mine = self.part(out, k, y, cut)
            came = arrived.at[k, cut, y]

            def up():
                return send(mine, mine, sent.at[0, q], came, r, lax.rem(c + m, n * m))

            def down():
                return send(mine, mine, sent.at[1, q], came, r, lax.rem(c + n * m - m, n * m))

            def side(d):
                return send(mine, mine, sent.at[1 + d, q], came, r, z * m + lax.rem(y + d, m))

            return up, down, side

        def own(cut):
            return x.at[span(cut, self.block[0] // cuts), :]

        def home(cut):
            return send(own(cut), self.part(out, r, y, cut), first.at[cut], arrived.at[r, cut, y], z, c)

        goes_up = jnp.logical_and(z >= r, z < n - 1)
        goes_down = jnp.logical_and(z <= r, z > 0)
        if phase == 0:

            @pl.when(r == z)
            def _():
                for cut in range(cuts):
                    pltpu.make_async_copy(own(cut), self.part(out, r, y, cut), arrived.at[r, cut, y]).start()

            @pl.when(r != z)
            def _():
                for cut in range(cuts):
                    home(cut).start()
        elif phase <= n * cuts:
            q = phase - 1
            await_bytes(self.part(out, q // cuts, y, q % cuts), arrived.at[q // cuts, q % cuts, y])
            up, down, side = moves(q)

            @pl.when(goes_up)
            def _():
                up().start()

            @pl.when(goes_down)
            def _():
                down().start()

            for d in range(1, m):
                side(d).start()
        else:
            for q in range(n * cuts):
                for d in range(1, m):
                    other = lax.rem(y + d, m)
                    await_bytes(self.part(out, q // cuts, other, q % cuts), arrived.at[q // cuts, q % cuts, other])
            for q in range(n * cuts):
                up, down, side = moves(q)

                @pl.when(goes_up)
                def _():
                    up().wait_send()

                @pl.when(goes_down)
                def _():
                    down().wait_send()

                for d in range(1, m):
                    side(d).wait_send()

            @pl.when(r != z)
            def _():
                for cut in range(cuts):
                    home(cut).wait_send()


class Fold:
    window = 6

    def __init__(self, n, m, block, by_frames, cuts):
        self.n, self.m, self.block, self.by_frames, self.cuts = n, m, block, by_frames, cuts
        self.out_shape = [jax.ShapeDtypeStruct(block, jnp.bfloat16)]
        self.out_specs = [VMEM]
        self.in_specs = [VMEM]
        piece = (block[0] // cuts, block[1])
        count = n * cuts
        self.scratch = [
            pltpu.VMEM((count, m) + piece, jnp.bfloat16),
            pltpu.VMEM((2, count) + piece, jnp.bfloat16),
            pltpu.VMEM((count,) + piece, jnp.bfloat16),
            DMA((count, m)),
            DMA((count, m)),
            DMA((2, count)),
            DMA((count,)),
            DMA((cuts,)),
        ]
        self.phases = count + 2

    part = Spread.part

    def run(self, phase, refs):
        parts, out, ybuf, zbuf, sbuf, ysent, ycame, zcame, zsent, ocame = refs
        n, m, cuts = self.n, self.m, self.cuts
        a, b = self.block
        high = a // cuts
        r, c = lax.axis_index("row"), lax.axis_index("col")
        z, y = c // m, c % m
        lower, upper = lax.rem(c + n * m - m, n * m), lax.rem(c + m, n * m)

        def side(q, d):
            other = lax.rem(y + d, m)
            mine = self.part(parts, q // cuts, other, q % cuts)
            return send(mine, ybuf.at[q, y], ysent.at[q, d], ycame.at[q, y], r, z * m + other)

        def onward(q):
            def down():
                return send(sbuf.at[q], zbuf.at[0, q], zsent.at[q], zcame.at[0, q], r, lower)

            def up():
                return send(sbuf.at[q], zbuf.at[1, q], zsent.at[q], zcame.at[1, q], r, upper)

            def home():
                cut = q % cuts
                return send(sbuf.at[q], out.at[span(cut, high), :], zsent.at[q], ocame.at[cut], q // cuts, c)

            return down, up, home

        if phase == 0:
            for q in range(min(self.window, n * cuts)):
                for d in range(1, m):
                    side(q, d).start()
        elif phase <= n * cuts:
            q = phase - 1
            k, cut = q // cuts, q % cuts
            for d in range(1, m):
                other = lax.rem(y + d, m)
                await_bytes(ybuf.at[q, other], ycame.at[q, other])
                side(q, d).wait_send()
                if q + self.window < n * cuts:
                    side(q + self.window, d).start()
            mine = self.part(parts, k, y, cut)

            def add(which):
                for w in which:
                    await_bytes(zbuf.at[w, q], zcame.at[w, q])

                def body(rows):
                    total = mine[rows, :].astype(jnp.float32)
                    for d in range(1, m):
                        total = total + ybuf[q, lax.rem(y + d, m), rows, :].astype(jnp.float32)
                    for w in which:
                        total = total + zbuf[w, q, rows, :].astype(jnp.float32)
                    sbuf[q, rows, :] = total.astype(jnp.bfloat16)

                by_rows(high, b, body)

            above = jnp.logical_and(z >= r, z < n - 1)
            below = jnp.logical_and(z <= r, z > 0)

            @pl.when(jnp.logical_and(above, below))
            def _():
                add((0, 1))

            @pl.when(jnp.logical_and(above, jnp.logical_not(below)))
            def _():
                add((0,))

            @pl.when(jnp.logical_and(jnp.logical_not(above), below))
            def _():
                add((1,))

            @pl.when(jnp.logical_not(jnp.logical_or(above, below)))
            def _():
                add(())

            down, up, home = onward(q)

            @pl.when(z > r)
            def _():
                down().start()

            @pl.when(z < r)
            def _():
                up().start()

            @pl.when(jnp.logical_and(z == r, r != k))
            def _():
                home().start()

            @pl.when(jnp.logical_and(z == r, r == k))
            def _():
                def keep(rows):
                    out.at[span(cut, high), :][rows, :] = sbuf[q, rows, :]

                by_rows(high, b, keep)
        else:

            @pl.when(z != r)
            def _():
                for cut in range(cuts):
                    await_bytes(out.at[span(cut, high), :], ocame.at[cut])

            for q in range(n * cuts):
                down, up, home = onward(q)

                @pl.when(jnp.logical_or(z != r, r != q // cuts))
                def _():
                    down().wait_send()


class Small:
    def __init__(self, n, n_col, block, over_col):
        self.n, self.n_col, self.over_col = n, n_col, over_col
        self.out_shape = [jax.ShapeDtypeStruct((n,) + block, jnp.float32)]
        self.out_specs = [VMEM]
        self.in_specs = [VMEM]
        self.scratch = [
            pltpu.VMEM((n_col,) + block, jnp.float32),
            pltpu.VMEM(block, jnp.float32),
            DMA((n_col,)),
            DMA((n_col,)),
            DMA((n,)),
            DMA((n,)),
        ]
        self.phases = 3

    def run(self, phase, refs):
        x, out, slots, total, csent, ccame, rsent, rcame = refs
        n, n_col = self.n, self.n_col
        r, c = lax.axis_index("row"), lax.axis_index("col")

        def to_col(d):
            return send(x, slots.at[c], csent.at[d], ccame.at[c], r, lax.rem(c + d, n_col))

        def to_row(d):
            return send(total, out.at[r], rsent.at[d], rcame.at[r], lax.rem(r + d, n), c)

        if phase == 0:
            if self.over_col:
                for d in range(1, n_col):
                    to_col(d).start()
        elif phase == 1:
            if self.over_col:
                slots[c] = x[...]
                for d in range(1, n_col):
                    other = lax.rem(c + d, n_col)
                    await_bytes(slots.at[other], ccame.at[other])
                value = slots[0]
                for j in range(1, n_col):
                    value = value + slots[j]
                total[...] = value
            else:
                total[...] = x[...]
            for d in range(1, n):
                to_row(d).start()
            out[r] = total[...]
        else:
            for d in range(1, n):
                other = lax.rem(r + d, n)
                await_bytes(out.at[other], rcame.at[other])
            for d in range(1, n):
                to_row(d).wait_send()
            if self.over_col:
                for d in range(1, n_col):
                    to_col(d).wait_send()


class RowFold:
    def __init__(self, n, block, by_frames, count):
        self.n, self.block, self.by_frames, self.count = n, block, by_frames, count
        half = n // 2
        self.out_shape = [jax.ShapeDtypeStruct(block, jnp.float32)] * count
        self.out_specs = [VMEM] * count
        self.in_specs = [VMEM] * count
        buf = pltpu.VMEM((count, half) + block, jnp.bfloat16)
        sem = DMA((count, half))
        self.scratch = [buf, buf, buf, sem, sem, sem, sem]
        self.phases = 3

    def part(self, ref, k):
        a, b = self.block
        return ref.at[span(k, a), :] if self.by_frames else ref.at[:, span(k, b)]

    def run(self, phase, refs):
        count = self.count
        parts, outs = refs[:count], refs[count : 2 * count]
        near, far, sums, nsent, ncame, fsent, fcame = refs[2 * count :]
        n = self.n
        half = n // 2
        a, b = self.block
        r, c = lax.axis_index("row"), lax.axis_index("col")
        x, core = r // 2, r % 2
        sibling = x * 2 + 1 - core

        def to_sibling(j, d):
            g = lax.rem(x + d, half)
            return send(
                self.part(parts[j], g * 2 + 1 - core), near.at[j, g], nsent.at[j, g], ncame.at[j, g], sibling, c
            )

        def across(j, d):
            g = lax.rem(x + d, half)
            return send(sums.at[j, g], far.at[j, x], fsent.at[j, g], fcame.at[j, x], g * 2 + core, c)

        order = list(range(1, half)) + [0]
        if phase == 0:
            for d in order:
                for j in range(count):
                    to_sibling(j, d).start()
        elif phase == 1:
            for d in range(1, half):
                g = lax.rem(x + d, half)
                for j in range(count):
                    await_bytes(near.at[j, g], ncame.at[j, g])
                    mine = self.part(parts[j], g * 2 + core)

                    def add(rows):
                        sums[j, g, rows, :] = (
                            mine[rows, :].astype(jnp.float32) + near[j, g, rows, :].astype(jnp.float32)
                        ).astype(jnp.bfloat16)

                    by_rows(a, b, add)
                    across(j, d).start()
        else:
            for j in range(count):
                await_bytes(near.at[j, x], ncame.at[j, x])
                for d in range(1, half):
                    g = lax.rem(x + d, half)
                    await_bytes(far.at[j, g], fcame.at[j, g])
                mine = self.part(parts[j], r)

                def total(rows):
                    value = mine[rows, :].astype(jnp.float32) + near[j, x, rows, :].astype(jnp.float32)
                    for d in range(1, half):
                        value = value + far[j, lax.rem(x + d, half), rows, :].astype(jnp.float32)
                    outs[j][rows, :] = value

                by_rows(a, b, total)
            for j in range(count):
                for d in order:
                    to_sibling(j, d).wait_send()
                for d in range(1, half):
                    across(j, d).wait_send()


class RowGather:
    late = True

    def __init__(self, n, block, by_frames, count):
        self.n, self.block, self.by_frames, self.count = n, block, by_frames, count
        a, b = block
        whole = (n * a, b) if by_frames else (a, n * b)
        half = n // 2
        self.out_shape = [jax.ShapeDtypeStruct(whole, jnp.bfloat16)] * count
        self.out_specs = [VMEM] * count
        self.in_specs = [ANY] * count
        self.scratch = [DMA((count, n)), DMA((count, half)), DMA((count, half)), DMA((count,))]
        self.phases = 3

    part = RowFold.part

    def run(self, phase, refs):
        count = self.count
        xs, outs = refs[:count], refs[count : 2 * count]
        came, fsent, nsent, kept = refs[2 * count :]
        n = self.n
        half = n // 2
        r, c = lax.axis_index("row"), lax.axis_index("col")
        x, core = r // 2, r % 2
        sibling = x * 2 + 1 - core

        def keep(j):
            return pltpu.make_async_copy(xs[j], self.part(outs[j], r), kept.at[j])

        def across(j, d):
            g = lax.rem(x + d, half)
            return send(xs[j], self.part(outs[j], r), fsent.at[j, d], came.at[j, r], g * 2 + core, c)

        def to_sibling(j, d):
            g = lax.rem(x + d, half)
            block = self.part(outs[j], g * 2 + core)
            source = xs[j] if d == 0 else block
            return send(source, block, nsent.at[j, d], came.at[j, g * 2 + core], sibling, c)

        if phase == 0:
            for j in range(count):
                for d in range(1, half):
                    across(j, d).start()
                to_sibling(j, 0).start()
                keep(j).start()
        elif phase == 1:
            for d in range(1, half):
                g = lax.rem(x + d, half)
                for j in range(count):
                    await_bytes(self.part(outs[j], g * 2 + core), came.at[j, g * 2 + core])
                    to_sibling(j, d).start()
        else:
            for j in range(count):
                for d in range(half):
                    g = lax.rem(x + d, half)
                    await_bytes(self.part(outs[j], g * 2 + 1 - core), came.at[j, g * 2 + 1 - core])
                keep(j).wait()
                for d in range(1, half):
                    across(j, d).wait_send()
                for d in range(half):
                    to_sibling(j, d).wait_send()


class Products:
    tile = 128

    def __init__(self, n, n_col, frames, depth, chans, steps):
        self.depth, self.chans = depth, chans
        grads = jax.ShapeDtypeStruct((depth, chans), jnp.float32)
        tiles = depth // self.tile
        self.small = Small(n, n_col, (tiles, self.tile), True)
        self.in_specs = [VMEM] + [ANY] * 4 + [VMEM] * 2
        self.out_shape = [grads] * 3 + self.small.out_shape
        self.out_specs = [VMEM] * 3 + self.small.out_specs
        self.scratch = [
            pltpu.VMEM((tiles, self.tile), jnp.float32),
            pltpu.VMEM((frames, depth), jnp.bfloat16),
            pltpu.VMEM((frames, chans), jnp.bfloat16),
            pltpu.VMEM((frames, chans), jnp.bfloat16),
            pltpu.VMEM((frames, chans), jnp.bfloat16),
            DMA((4,)),
        ] + self.small.scratch
        self.phases = steps
        work = [("both", i) for i in range(tiles)] + [("small", 0)]
        work += [("out", i) for i in range(tiles)]
        work.insert(tiles + 3, ("small", 1))
        self.work = {}
        for place, item in enumerate(work):
            self.work.setdefault(1 + place * (steps - 2) // len(work), []).append(item)
        self.work[steps - 1] = [("small", 2)]

    def run(self, phase, refs):
        normed, w_value, w_gate = refs[0], refs[5], refs[6]
        g_value, g_gate, g_out, gain_out = refs[7:11]
        gain_sum, act, grad, value, gate, loaded = refs[11:17]
        tile = self.tile

        def load(j):
            return pltpu.make_async_copy(refs[1 + j], refs[12 + j], loaded.at[j])

        if phase == 0:
            for j in (2, 3, 1, 0):
                load(j).start()
        elif phase == 1:
            for j in range(4):
                load(j).wait()
        for kind, i in self.work.get(phase, []):
            here = pl.ds(i * tile, tile)
            if kind == "small":
                self.small.run(i, (gain_sum, gain_out) + tuple(refs[17:]))
            elif kind == "both":
                left = normed[:, here]
                first = dot(left, value[...], (0, 0))
                g_value[here, :] = first
                total = first * w_value[here, :].astype(jnp.float32)
                second = dot(left, gate[...], (0, 0))
                g_gate[here, :] = second
                total = total + second * w_gate[here, :].astype(jnp.float32)
                narrow = total[:, :tile]
                for j in range(1, self.chans // tile):
                    narrow = narrow + total[:, j * tile : (j + 1) * tile]
                gain_sum[pl.ds(i, 1), :] = jnp.sum(narrow.T, axis=0, keepdims=True)
            else:
                g_out[here, :] = dot(act[:, here], grad[...], (0, 0))


def greet(n, n_col):
    r, c = lax.axis_index("row"), lax.axis_index("col")
    barrier = pltpu.get_barrier_semaphore()

    def hello(row, col):
        pl.semaphore_signal(barrier, inc=1, device_id=(row, col), device_id_type=MESH)

    for d in range(1, n):
        hello(lax.rem(r + d, n), c)
    for d in range(1, n_col):
        hello(r, lax.rem(c + d, n_col))
    pl.semaphore_wait(barrier, n - 1 + n_col - 1)


def exchange(n, m, ident, moves, operands):
    in_specs = [s for mv in moves for s in mv.in_specs]
    out_specs = [s for mv in moves for s in mv.out_specs]
    out_shape = [s for mv in moves for s in mv.out_shape]
    scratch = [s for mv in moves for s in mv.scratch]

    def body(*refs):
        ins = refs[: len(in_specs)]
        outs = refs[len(in_specs) : len(in_specs) + len(out_specs)]
        rest = refs[len(in_specs) + len(out_specs) :]
        own = []
        i = o = s = 0
        for mv in moves:
            own.append(
                tuple(ins[i : i + len(mv.in_specs)])
                + tuple(outs[o : o + len(mv.out_specs)])
                + tuple(rest[s : s + len(mv.scratch)])
            )
            i, o, s = i + len(mv.in_specs), o + len(mv.out_specs), s + len(mv.scratch)
        greet(n, n * m)
        steps = max(mv.phases for mv in moves)
        for step in range(steps):
            for mv, mine in zip(moves, own):
                late = getattr(mv, "late", False) and steps > mv.phases
                at = {0: 0, (steps // 2 if late else 1): 1, steps - 1: 2}
                if mv.phases == steps:
                    mv.run(step, mine)
                elif step in at:
                    mv.run(at[step], mine)

    return pl.pallas_call(
        body,
        out_shape=out_shape,
        in_specs=in_specs,
        out_specs=out_specs,
        scratch_shapes=scratch,
        compiler_params=pltpu.CompilerParams(
            collective_id=ident, has_side_effects=True, vmem_limit_bytes=50 * 2**20
        ),
        cost_estimate=pl.CostEstimate(flops=0, bytes_accessed=100_000_000, transcendentals=0),
    )(*operands)


def dot(left, right, contract):
    return lax.dot_general(left, right, ((contract[:1], contract[1:]), ((), ())), preferred_element_type=jnp.float32)


def eight(block):
    return jnp.pad(block, ((0, 8 - block.shape[0]), (0, 0)))


def clips(total):
    return [(start, min(start + LEN, total)) for start in range(0, total, LEN)]


def padded(block):
    return jnp.pad(block, ((HALF, HALF), (0, 0)))


def shards(frames, gain, w_value, w_gate, kernel, bias, w_out, grad_out):
    n, n_col = lax.axis_size("row"), lax.axis_size("col")
    m = n_col // n
    rows, feats = frames.shape
    depth, chans = w_value.shape
    total, width = rows * n, feats * n_col
    own = chans // n
    r, c = lax.axis_index("row"), lax.axis_index("col")

    wide = frames.astype(jnp.float32)
    sums = eight(jnp.stack([jnp.sum(wide, axis=1), jnp.sum(wide * wide, axis=1)]))
    frames_full, grad_full, sums = exchange(
        n,
        m,
        1,
        [
            Spread(n, m, (rows, feats), True, 4),
            RowGather(n, (rows, feats), True, 1),
            Small(n, n_col, (8, rows), True),
        ],
        (frames, grad_out, sums),
    )
    mean = sums[:, 0].reshape(total) / width
    inv_std = lax.rsqrt(sums[:, 1].reshape(total) / width - mean * mean + epsilon)
    gain_row = lax.dynamic_slice_in_dim(gain, r * depth, depth, 0)
    normed = (
        (frames_full.astype(jnp.float32) - mean[:, None]) * inv_std[:, None] * gain_row[None, :]
    ).astype(jnp.bfloat16)
    value_part = dot(normed, w_value, (1, 0)).astype(jnp.bfloat16)
    gate_part = dot(normed, w_gate, (1, 0)).astype(jnp.bfloat16)
    act_part = dot(grad_full, w_out, (1, 1)).astype(jnp.bfloat16)
    pieces, left = [], gain_row
    for _ in range(3):
        piece = lax.reduce_precision(left, 8, 7)
        pieces.append(piece.astype(jnp.bfloat16))
        left = left - piece
    pieces = eight(jnp.stack(pieces))
    scaled = jnp.stack(
        [jnp.sum(dot(pieces, w_value, (1, 0)), axis=0), jnp.sum(dot(pieces, w_gate, (1, 0)), axis=0)]
    )

    value_pre, gate_pre, act_grad, scaled = exchange(
        n,
        m,
        2,
        [
            RowFold(n, (total, own), False, 2),
            Fold(n, m, (total, own), False, 4),
            Small(n, n_col, (8, chans), False),
        ],
        (value_part, gate_part, act_part, eight(scaled)),
    )
    scaled = lax.dynamic_slice_in_dim(jnp.sum(scaled, axis=0), r * own, own, 1)
    gate_sig = jax.nn.sigmoid(gate_pre)
    gated = (value_pre * gate_sig).astype(jnp.bfloat16).astype(jnp.float32)
    taps = lax.dynamic_slice_in_dim(kernel, r * own, own, 1)
    own_bias = lax.dynamic_slice_in_dim(bias, r * own, own, 0)
    conv_parts, glu_parts = [], []
    for begin, end in clips(total):
        ahead = padded(gated[begin:end])
        conv = jnp.zeros((end - begin, own), jnp.float32) + own_bias[None, :]
        for k in range(K):
            conv = conv + taps[k][None, :] * ahead[k : k + end - begin]
        conv_parts.append(conv)
    conv_pre = jnp.concatenate(conv_parts, axis=0)
    conv_sig = jax.nn.sigmoid(conv_pre)
    activated = (conv_pre * conv_sig).astype(jnp.bfloat16)
    conv_grad = (
        act_grad.astype(jnp.float32) * conv_sig * (1.0 + conv_pre * (1.0 - conv_sig))
    ).astype(jnp.bfloat16)
    conv_wide = conv_grad.astype(jnp.float32)
    tap_grads = jnp.zeros((K, own), jnp.float32)
    for begin, end in clips(total):
        back = padded(conv_wide[begin:end])
        ahead = padded(gated[begin:end])
        glu = jnp.zeros((end - begin, own), jnp.float32)
        tap_rows = []
        for k in range(K):
            glu = glu + taps[k][None, :] * back[2 * HALF - k : 2 * HALF - k + end - begin]
            tap_rows.append(jnp.sum(conv_wide[begin:end] * ahead[k : k + end - begin], axis=0))
        glu_parts.append(glu)
        tap_grads = tap_grads + jnp.stack(tap_rows)
    glu_grad = jnp.concatenate(glu_parts, axis=0)
    value_grad = (glu_grad * gate_sig).astype(jnp.bfloat16)
    gate_grad = (glu_grad * value_pre * gate_sig * (1.0 - gate_sig)).astype(jnp.bfloat16)
    bias_grad = jnp.sum(conv_wide, axis=0)
    depthwise = jnp.concatenate([tap_grads, bias_grad[None, :]], axis=0)
    value_wide, gate_wide = value_grad.astype(jnp.float32), gate_grad.astype(jnp.float32)
    norm_sums = jnp.stack(
        [
            jnp.sum(value_wide * scaled[0][None, :] + gate_wide * scaled[1][None, :], axis=1),
            jnp.sum(value_wide * value_pre + gate_wide * gate_pre, axis=1),
        ]
    )
    act_full, value_full, gate_full, norm_sums, depthwise = exchange(
        n,
        m,
        3,
        [
            Spread(n, m, (total, own), False, 4),
            RowGather(n, (total, own), False, 2),
            Small(n, n_col, (8, total), True),
            Small(n, n_col, (K + 1, own), False),
        ],
        (activated, value_grad, gate_grad, eight(norm_sums), depthwise),
    )
    norm_sums = jnp.sum(norm_sums, axis=0)[:2]
    depthwise = jnp.transpose(depthwise, (1, 0, 2)).reshape(K + 1, chans)
    out_part = dot(act_full, w_out, (1, 0)).astype(jnp.bfloat16)
    norm_part = (dot(value_full, w_value, (1, 1)) + dot(gate_full, w_gate, (1, 1))).astype(jnp.bfloat16)
    fold = Fold(n, m, (rows, feats), True, 4)
    out_sum, normed_grad, grad_value, grad_gate, grad_out_weight, gain_rows = exchange(
        n,
        m,
        4,
        [
            RowFold(n, (rows, feats), True, 1),
            fold,
            Products(n, n_col, total, depth, chans, fold.phases),
        ],
        (out_part, norm_part, normed, act_full, grad_full, value_full, gate_full, w_value, w_gate),
    )
    grad_gain = lax.dynamic_slice_in_dim(gain_rows.reshape(n * depth) / gain, c * feats, feats, 0)

    encoded = (wide + out_sum).astype(jnp.bfloat16)
    local_mean = lax.dynamic_slice_in_dim(mean, r * rows, rows, 0)
    local_inv = lax.dynamic_slice_in_dim(inv_std, r * rows, rows, 0)
    local_sums = lax.dynamic_slice_in_dim(norm_sums, r * rows, rows, 1) / width
    centred = (wide - local_mean[:, None]) * local_inv[:, None]
    local_gain = lax.dynamic_slice_in_dim(gain, c * feats, feats, 0)
    hat_grad = normed_grad.astype(jnp.float32) * local_gain[None, :]
    input_grad = (
        grad_out.astype(jnp.float32)
        + local_inv[:, None] * (hat_grad - local_sums[0][:, None] - centred * local_sums[1][:, None])
    ).astype(jnp.bfloat16)
    return (
        encoded,
        input_grad,
        grad_value,
        grad_gate,
        depthwise[:K],
        depthwise[K],
        grad_out_weight,
        grad_gain,
    )


def extended(block, sides, width):
    for axis, dim in sides:
        count = lax.axis_size(axis)
        forward = [(i, i + 1) for i in range(count - 1)]
        backward = [(target, source) for source, target in forward]
        low = lax.ppermute(
            lax.slice_in_dim(block, block.shape[dim] - width, None, axis=dim), axis, forward
        )
        high = lax.ppermute(lax.slice_in_dim(block, 0, width, axis=dim), axis, backward)
        block = jnp.concatenate([low, block, high], axis=dim)
    return block


def tap_masks(positions):
    offsets = jnp.arange(K, dtype=jnp.int32) - K // 2
    placed = (positions % LEN)[None, :] + offsets[:, None]
    return ((placed >= 0) & (placed < LEN)).astype(jnp.float32)


def contract_rows(left, right):
    return lax.dot_general(
        left, right, (((0,), (0,)), ((), ())), preferred_element_type=jnp.float32
    )


def contract_cols(left, right):
    return lax.dot_general(
        left, right, (((1,), (1,)), ((), ())), preferred_element_type=jnp.float32
    )


def narrow_shards(frames, gain, w_value, w_gate, kernel, bias, w_out, grad_out):
    row_count = frames.shape[0]
    col_count = frames.shape[1]
    chan_count = w_value.shape[1]
    width = col_count * lax.axis_size("col")
    half_width = K // 2
    row_start = lax.axis_index("row") * row_count
    col_start = lax.axis_index("col") * col_count
    local_gain = lax.dynamic_slice_in_dim(gain, col_start, col_count, 0)
    wide = frames.astype(jnp.float32)
    sum_row, square_sum = lax.psum((jnp.sum(wide, axis=1), jnp.sum(wide * wide, axis=1)), "col")
    mean_row = sum_row / width
    inv_std = lax.rsqrt(square_sum / width - mean_row * mean_row + epsilon)
    centred = (wide - mean_row[:, None]) * inv_std[:, None]
    normed = lax.all_gather(
        (centred * local_gain[None, :]).astype(jnp.bfloat16), "col", axis=1, tiled=True
    )
    value_full, gate_full = (
        lax.all_gather(w_value, "row", axis=0, tiled=True),
        lax.all_gather(w_gate, "row", axis=0, tiled=True),
    )
    value_pre = jnp.dot(normed, value_full, preferred_element_type=jnp.float32)
    gate_pre = jnp.dot(normed, gate_full, preferred_element_type=jnp.float32)
    gate_sig = jax.nn.sigmoid(gate_pre)
    gated = (value_pre * gate_sig).astype(jnp.bfloat16)
    padded_glu = extended(gated, (("row", 0),), half_width).astype(jnp.float32)
    local_masks = tap_masks(row_start + jnp.arange(row_count, dtype=jnp.int32))
    conv_pre = jnp.zeros((row_count, chan_count), jnp.float32) + bias[None, :]
    for tap_index in range(K):
        conv_pre = (
            conv_pre
            + kernel[tap_index][None, :]
            * local_masks[tap_index][:, None]
            * padded_glu[tap_index : tap_index + row_count]
        )
    conv_sig = jax.nn.sigmoid(conv_pre)
    activated = (conv_pre * conv_sig).astype(jnp.bfloat16)
    act_full = lax.all_gather(activated, "col", axis=1, tiled=True)
    out_full = lax.all_gather(w_out, "row", axis=0, tiled=True)
    encoded = (
        frames.astype(jnp.float32) + jnp.dot(act_full, out_full, preferred_element_type=jnp.float32)
    ).astype(jnp.bfloat16)
    act_terms = contract_cols(grad_out, out_full)
    act_grad = lax.psum_scatter(
        act_terms.astype(jnp.bfloat16), "col", scatter_dimension=1, tiled=True
    ).astype(jnp.float32)
    grad_out_weight = lax.psum_scatter(
        contract_rows(act_full, grad_out).astype(jnp.bfloat16),
        "row",
        scatter_dimension=0,
        tiled=True,
    ).astype(jnp.float32)
    conv_grad = (act_grad * conv_sig * (1.0 + conv_pre * (1.0 - conv_sig))).astype(jnp.bfloat16)
    conv_wide = conv_grad.astype(jnp.float32)
    padded_grad = extended(conv_grad, (("row", 0),), half_width).astype(jnp.float32)
    outer_masks = tap_masks(
        row_start - half_width + jnp.arange(row_count + 2 * half_width, dtype=jnp.int32)
    )
    glu_grad = jnp.zeros((row_count, chan_count), jnp.float32)
    kernel_rows = []
    for tap_index in range(K):
        begin = 2 * half_width - tap_index
        glu_grad = (
            glu_grad
            + kernel[tap_index][None, :]
            * outer_masks[tap_index, begin : begin + row_count][:, None]
            * padded_grad[begin : begin + row_count]
        )
        kernel_rows.append(
            jnp.sum(
                local_masks[tap_index][:, None]
                * conv_wide
                * padded_glu[tap_index : tap_index + row_count],
                axis=0,
            )
        )
    kernel_term = jnp.stack(kernel_rows)
    bias_term = jnp.sum(conv_wide, axis=0)
    grad_kernel, grad_bias = lax.psum((kernel_term, bias_term), "row")
    value_grad = (glu_grad * gate_sig).astype(jnp.bfloat16)
    gate_grad = (glu_grad * value_pre * gate_sig * (1.0 - gate_sig)).astype(jnp.bfloat16)
    both_grads = jnp.concatenate([value_grad, gate_grad], axis=1)
    in_weight = lax.psum_scatter(
        contract_rows(normed, both_grads).astype(jnp.bfloat16),
        "row",
        scatter_dimension=0,
        tiled=True,
    ).astype(jnp.float32)
    grad_value = in_weight[:, :chan_count]
    grad_gate = in_weight[:, chan_count:]
    norm_terms = contract_cols(value_grad, value_full) + contract_cols(gate_grad, gate_full)
    normed_grad = lax.psum_scatter(
        norm_terms.astype(jnp.bfloat16), "col", scatter_dimension=1, tiled=True
    ).astype(jnp.float32)
    hat_grad = normed_grad * local_gain[None, :]
    first_sum, second_sum = lax.psum(
        (jnp.sum(hat_grad, axis=1), jnp.sum(hat_grad * centred, axis=1)), "col"
    )
    input_grad = (
        grad_out.astype(jnp.float32)
        + inv_std[:, None]
        * (hat_grad - first_sum[:, None] / width - centred * (second_sum / width)[:, None])
    ).astype(jnp.bfloat16)
    gain_term = jnp.sum(normed_grad * centred, axis=0)
    grad_gain = lax.psum(gain_term, "row")
    return (
        encoded,
        input_grad,
        grad_value,
        grad_gate,
        grad_kernel,
        grad_bias,
        grad_out_weight,
        grad_gain,
    )


def choose(frames, gain, w_value, *others):
    fits = w_value.shape[1] % (128 * lax.axis_size("row")) == 0 and lax.axis_size("col") % lax.axis_size("row") == 0
    return (shards if fits else narrow_shards)(frames, gain, w_value, *others)


def solution(mesh):
    tile = P("row", "col")
    return jax.shard_map(
        choose,
        mesh=mesh,
        in_specs=(tile, P(), tile, tile, P(None, "col"), P("col"), tile, tile),
        out_specs=(tile, tile, tile, tile, P(None, "col"), P("col"), tile, P("col")),
        check_vma=False,
    )
```

profile of v0, /device:TPU:0, one launch (start us, length us, event | category | flops | bytes accessed | tf_op | source)
XLA Modules:
  0.0 306.2 jit_solution(596663772226464129)
XLA Ops:
  0.7 1.5 dynamic_slice.27
  2.1 1.7 fusion.67
  3.8 1.2 convert_reduce_fusion.1
  5.8 1.5 convolution_reduce_fusion.1
  7.3 1.5 convolution_reduce_fusion
  8.8 47.0 %shard_map.143 = (bf16[1536,1024]{1,0:T(8,128)(2,1)}, bf16[1536,512]{1,0:T(8,128)(2,1)S(1)}, f32[4,8,384]{2,1,0:T(8,128)S(1)}) custom-call(bf16[384,512]{1,0:T(8,128)(2,1)S(1)} %copy-done.3, bf16[384,512]{1,0:T(8,128)(2,1)S(1)} %copy-done.10, f32[8,384]{1,0:T(8,128)S(1)} %select_maximum_fusion.2.refs_2_), custom_call_target="tpu_custom_call" | custom-call | bytes 100000000 | tf_op jit(solution)/shard_map/pallas_call | solution.py:587
  55.8 1.1 copy-done.6
  57.7 2.6 multiply_convert_fusion.refs_2_
  61.2 2.9 convolution_convert_fusion.2.refs_1_
  64.1 1.8 convolution_convert_fusion.3.refs_0_
  65.9 3.5 %convolution_convert_fusion.refs_2_ = bf16[1536,1024]{1,0:T(8,128)(2,1)} fusion(bf16[1536,512]{1,0:T(8,128)(2,1)S(1)} %copy-done.7, bf16[1024,512]{1,0:T(8,128)(2,1)S(1)} %copy-done), kind=kOutput, calls=%fused_computation.35 | convolution fusion | flops 1612185600 | bytes 5767168 | tf_op jit(solution)/shard_map/dot_general | solution.py:601
  69.5 62.1 %shard_map.144 = (f32[1536,128]{1,0:T(8,128)S(1)}, f32[1536,128]{1,0:T(8,128)S(1)}, bf16[1536,128]{1,0:T(8,128)(2,1)S(1)}, f32[4,8,512]{2,1,0:T(8,128)S(1)}) custom-call(bf16[1536,512]{1,0:T(8,128)(2,1)S(1)} %convolution_convert_fusion.3.refs_0_, bf16[1536,512]{1,0:T(8,128)(2,1)} %convolution_convert_fusion.2.refs_1_, ...), custom_call_target="tpu_custom_call" | custom-call | bytes 100000000 | tf_op jit(solution)/shard_map/pallas_call | solution.py:587
  135.6 1.5 dynamic-slice_bitcast_fusion.29
  137.2 1.6 fusion.59
  138.8 7.1 %fusion.57 = (f32[128]{0:T(128)}, f32[128]{0:T(128)}, f32[128]{0:T(128)}, f32[128]{0:T(128)}, f32[128]{0:T(128)}, /*index=5*/f32[128]{0:T(128)}, f32[128]{0:T(12...) fusion(f32[1536,128]{1,0:T(8,128)S(1)} %fusion.59, ...), kind=kLoop, calls=%fused_computation.106 | loop fusion | flops 19659008 | bytes 2382848 | tf_op jit(solution)/shard_map/reduce_sum | solution.py:695
  145.9 2.5 fusion.58
  148.5 2.9 concatenate.3.refs_4_
  151.3 1.3 multiply_convert_fusion.4.refs_0_
  153.7 5.2 %fusion.1 = (f32[1536]{0:T(1024)S(1)}, f32[1536]{0:T(1024)S(1)}, bf16[1536,128]{1,0:T(8,128)(2,1)S(1)}, bf16[1536,128]{1,0:T(8,128)(2,1)S(1)}) fusion(f32[128]{0:T(128)} %get-tuple-element.129, f32[128]{0:T(128)} %get-tuple-element.130, f32[1536,128]{1,0:T(8,128)} %copy-done.5, f32[1536,128]{1,0:T(8,128)} %copy-done.4, f32[128]{0:T(128)} %copy-done.36, ...), kind=kLoop, calls=%fused_computation.50 | loop fusion | flops 16118784 | bytes 3568128 | tf_op jit(solution)/shard_map/reduce_sum | solution.py:706
  159.0 47.6 %shard_map.145 = (bf16[1536,1024]{1,0:T(8,128)(2,1)}, bf16[1536,512]{1,0:T(8,128)(2,1)S(1)}, bf16[1536,512]{1,0:T(8,128)(2,1)}, f32[4,8,1536]{2,1,0:T(8,128)S(1)}, f32[4,32,128]{2,1,0:T(8,128)S(1)}) custom-call(bf16[1536,128]{1,0:T(8,128)(2,1)S(1)} %multiply_convert_fusion.4.refs_0_, bf16[1536,128]{1,0:T(8,128)(2,1)S(1)} %get-tuple-element.89.refs_1_, ...), custom_call_target="tpu_custom_call" | custom-call | bytes 100000000 | tf_op jit(solution)/shard_map/pallas_call | solution.py:587
  206.6 1.1 copy-done.8
  209.0 1.6 reduce_sum.399
  211.4 1.3 slice.473
  214.3 5.0 %convolution_convert_fusion.1.refs_0_ = bf16[1536,512]{1,0:T(8,128)(2,1)} fusion(bf16[1536,1024]{1,0:T(8,128)(2,1)} %get-tuple-element.33.refs_3_, bf16[1024,512]{1,0:T(8,128)(2,1)S(1)} %copy-done), kind=kOutput, calls=%fused_computation.36 | convolution fusion | flops 1611399168 | bytes 5767168 | tf_op jit(solution)/shard_map/dot_general | solution.py:601
  219.2 1.9 fusion.70
  221.1 3.6 %add_convert_fusion.refs_1_ = bf16[1536,1024]{1,0:T(8,128)(2,1)} fusion(f32[1536,1024]{1,0:T(8,128)S(1)} %fusion.70, bf16[1536,512]{1,0:T(8,128)(2,1)S(1)} %copy-done.17, bf16[1024,512]{1,0:T(8,128)(2,1)S(1)} %copy-done.1), kind=kOutput, calls=%fused_computation.33 | convolution fusion | flops 1613758464 | bytes 12058624 | tf_op jit(solution)/shard_map/dot_general | solution.py:601
  224.8 73.6 %shard_map.146 = (f32[384,512]{1,0:T(8,128)S(1)}, bf16[384,512]{1,0:T(8,128)(2,1)S(1)}, f32[1024,512]{1,0:T(8,128)}, f32[1024,512]{1,0:T(8,128)}, f32[1024,512]{1,0:T(8,128)}, /*index=5*/f32[4,8,128]{2,1,0:T(8,128)S(1)}) custom-call(bf16[1536,512]{1,0:T(8,128)(2,1)} %convolution_convert_fusion.1.refs_0_, bf16[1536,1024]{1,0:T(8,128)(2,1)} %add_convert_fusion.refs_1_, ...), custom_call_target="tpu_custom_call" | custom-call | bytes 100000000 | tf_op jit(solution)/shard_map/pallas_call | solution.py:587
  298.4 1.5 dynamic-slice_divide_fusion
  300.0 1.2 fusion.11
  301.2 1.3 copy.21
  302.5 1.3 copy.22
  304.9 1.3 copy.23
  (99 shorter events, 12.1 us)
Async XLA Ops:
  0.6 65.3 %copy-start = (bf16[1024,512]{1,0:T(8,128)(2,1)S(1)}, bf16[1024,512]{1,0:T(8,128)(2,1)}, u32[]{:S(2)}) copy-start(bf16[1024,512]{1,0:T(8,128)(2,1)} %param.14) | copy-start | bytes 3145732
  0.6 8.2 %copy-start.3 = (bf16[384,512]{1,0:T(8,128)(2,1)S(1)}, bf16[384,512]{1,0:T(8,128)(2,1)}, u32[]{:S(2)}) copy-start(bf16[384,512]{1,0:T(8,128)(2,1)} %refs_0_.1) | copy-start | bytes 1179652
  0.7 8.2 %copy-start.10 = (bf16[384,512]{1,0:T(8,128)(2,1)S(1)}, bf16[384,512]{1,0:T(8,128)(2,1)}, u32[]{:S(2)}) copy-start(bf16[384,512]{1,0:T(8,128)(2,1)} %refs_1_.1) | copy-start | bytes 1179652
  55.8 1.1 copy-start.6
  57.7 3.4 %copy-start.1 = (bf16[1024,512]{1,0:T(8,128)(2,1)S(1)}, bf16[1024,512]{1,0:T(8,128)(2,1)}, u32[]{:S(2)}) copy-start(bf16[1024,512]{1,0:T(8,128)(2,1)} %refs_8_.1) | copy-start | bytes 3145732
  60.4 3.7 %copy-start.16 = (bf16[1536,1024]{1,0:T(8,128)(2,1)}, bf16[1536,1024]{1,0:T(8,128)(2,1)S(1)}, u32[]{:S(2)}) copy-start(bf16[1536,1024]{1,0:T(8,128)(2,1)S(1)} %multiply_convert_fusion.refs_2_) | copy-start | bytes 9437188
  61.2 2.9 copy-start.2
  64.1 1.8 copy-start.7
  131.6 0.9 copy-start.4
  137.1 11.2 %copy-start.24 = (f32[128]{0:T(128)}, f32[128]{0:T(128)S(1)}, u32[]{:S(2)}) copy-start(f32[128]{0:T(128)S(1)} %get-tuple-element.112) | copy-start | bytes 1540
  137.1 11.2 %copy-start.25 = (f32[128]{0:T(128)}, f32[128]{0:T(128)S(1)}, u32[]{:S(2)}) copy-start(f32[128]{0:T(128)S(1)} %get-tuple-element.113) | copy-start | bytes 1540
  137.1 11.2 %copy-start.26 = (f32[128]{0:T(128)}, f32[128]{0:T(128)S(1)}, u32[]{:S(2)}) copy-start(f32[128]{0:T(128)S(1)} %get-tuple-element.114) | copy-start | bytes 1540
  137.1 11.2 %copy-start.27 = (f32[128]{0:T(128)}, f32[128]{0:T(128)S(1)}, u32[]{:S(2)}) copy-start(f32[128]{0:T(128)S(1)} %get-tuple-element.115) | copy-start | bytes 1540
  137.1 11.2 %copy-start.28 = (f32[128]{0:T(128)}, f32[128]{0:T(128)S(1)}, u32[]{:S(2)}) copy-start(f32[128]{0:T(128)S(1)} %get-tuple-element.116) | copy-start | bytes 1540
  137.1 11.2 %copy-start.29 = (f32[128]{0:T(128)}, f32[128]{0:T(128)S(1)}, u32[]{:S(2)}) copy-start(f32[128]{0:T(128)S(1)} %get-tuple-element.117) | copy-start | bytes 1540
  137.1 11.2 %copy-start.30 = (f32[128]{0:T(128)}, f32[128]{0:T(128)S(1)}, u32[]{:S(2)}) copy-start(f32[128]{0:T(128)S(1)} %get-tuple-element.118) | copy-start | bytes 1540
  137.2 11.2 %copy-start.31 = (f32[128]{0:T(128)}, f32[128]{0:T(128)S(1)}, u32[]{:S(2)}) copy-start(f32[128]{0:T(128)S(1)} %get-tuple-element.119) | copy-start | bytes 1540
  137.2 11.2 %copy-start.32 = (f32[128]{0:T(128)}, f32[128]{0:T(128)S(1)}, u32[]{:S(2)}) copy-start(f32[128]{0:T(128)S(1)} %get-tuple-element.120) | copy-start | bytes 1540
  137.2 11.2 %copy-start.33 = (f32[128]{0:T(128)}, f32[128]{0:T(128)S(1)}, u32[]{:S(2)}) copy-start(f32[128]{0:T(128)S(1)} %get-tuple-element.121) | copy-start | bytes 1540
  137.2 11.2 %copy-start.34 = (f32[128]{0:T(128)}, f32[128]{0:T(128)S(1)}, u32[]{:S(2)}) copy-start(f32[128]{0:T(128)S(1)} %get-tuple-element.122) | copy-start | bytes 1540
  137.2 11.2 %copy-start.35 = (f32[128]{0:T(128)}, f32[128]{0:T(128)S(1)}, u32[]{:S(2)}) copy-start(f32[128]{0:T(128)S(1)} %get-tuple-element.123) | copy-start | bytes 1540
  137.2 11.2 %copy-start.36 = (f32[128]{0:T(128)}, f32[128]{0:T(128)S(1)}, u32[]{:S(2)}) copy-start(f32[128]{0:T(128)S(1)} %get-tuple-element.124) | copy-start | bytes 1540
  145.9 2.6 copy-start.18
  206.6 1.1 copy-start.8
  214.3 5.0 %copy-start.9 = (bf16[1536,512]{1,0:T(8,128)(2,1)S(1)}, bf16[1536,512]{1,0:T(8,128)(2,1)}, u32[]{:S(2)}) copy-start(bf16[1536,512]{1,0:T(8,128)(2,1)} %copy-done.8) | copy-start | bytes 4718596
  219.2 1.9 copy-start.17
  224.8 75.2 %copy-start.11 = (bf16[384,512]{1,0:T(8,128)(2,1)S(1)}, bf16[384,512]{1,0:T(8,128)(2,1)}, u32[]{:S(2)}) copy-start(bf16[384,512]{1,0:T(8,128)(2,1)} %refs_1_.1) | copy-start | bytes 1179652
  224.8 75.2 %copy-start.22 = (f32[384]{0:T(512)S(1)}, f32[384]{0:T(512)}, u32[]{:S(2)}) copy-start(f32[384]{0:T(512)} %dynamic_slice.34) | copy-start | bytes 4612
  224.8 75.2 %copy-start.23 = (f32[384]{0:T(512)S(1)}, f32[384]{0:T(512)}, u32[]{:S(2)}) copy-start(f32[384]{0:T(512)} %dynamic_slice.31) | copy-start | bytes 4612
  298.4 2.7 copy-start.21
  300.0 2.6 copy-start.20
  302.5 2.3 copy-start.19
  (5 other events, 3.6 us)
where the time goes:
time: 307 us; the launch traced here: 306 us
  Pallas kernels  230 us (75%)
  other arithmetic  28.5 us (9%)
  local copies, waits for them, and re-layouts  24.5 us (8%)
  matrix products  21.7 us (7%)
    pallas_call x4, Pallas kernels, exchange(): pl.pallas_call(body, out_shape=out_shape, in_specs=in_specs, out_specs=ou...  230 us
    dot_general x8, matrix products, dot(): lax.dot_general(left, right, ((contract[:1], contract[1:]), ((), ())), pr...  21.7 us
    unnamed x79, local copies, waits for them, and re-layouts  12.5 us
    reduce_sum x2, other arithmetic, shards(): jnp.sum(conv_wide[begin:end] * ahead[k:k + end - begin], axis=0)  9.53 us

commit v1 on v0

--- a/solution.py
+++ b/solution.py
@@ -609,8 +609,79 @@
     return [(start, min(start + LEN, total)) for start in range(0, total, LEN)]
 
 
-def padded(block):
-    return jnp.pad(block, ((HALF, HALF), (0, 0)))
+def sigmoid(value):
+    return 1.0 / (1.0 + jnp.exp(-value))
+
+
+def conv_body(bounds, value, gate, act_grad, taps, bias, act, v_grad, g_grad, tap_grads, ahead, back):
+    high, edge = 32, 16
+    wide = value.shape[1]
+    blank = jnp.zeros((edge, wide), jnp.float32)
+    tap_grads[...] = jnp.zeros_like(tap_grads)
+    for begin, end in bounds:
+        length = end - begin
+        for buffer in (ahead, back):
+            buffer[pl.ds(0, edge), :] = blank
+            buffer[pl.ds(edge + length, edge), :] = blank
+
+        @pl.loop(0, length // high)
+        def _(i):
+            rows = pl.ds(pl.multiple_of(begin + i * high, high), high)
+            inner = pl.ds(pl.multiple_of(edge + i * high, edge), high)
+            gated = value[rows, :] * sigmoid(gate[rows, :])
+            ahead[inner, :] = gated.astype(jnp.bfloat16).astype(jnp.float32)
+
+        @pl.loop(0, length // high)
+        def _(i):
+            start = pl.multiple_of(i * high, high)
+            rows = pl.ds(pl.multiple_of(begin + i * high, high), high)
+            inner = pl.ds(pl.multiple_of(edge + i * high, edge), high)
+            conv = jnp.broadcast_to(bias[pl.ds(0, 1), :], (high, wide))
+            for k in range(K):
+                conv = conv + taps[pl.ds(k, 1), :] * ahead[pl.ds(start + (edge - HALF + k), high), :]
+            sig = sigmoid(conv)
+            act[rows, :] = (conv * sig).astype(jnp.bfloat16)
+            grad = act_grad[rows, :].astype(jnp.float32) * sig * (1.0 + conv * (1.0 - sig))
+            back[inner, :] = grad.astype(jnp.bfloat16).astype(jnp.float32)
+
+        @pl.loop(0, length // high)
+        def _(i):
+            start = pl.multiple_of(i * high, high)
+            rows = pl.ds(pl.multiple_of(begin + i * high, high), high)
+            glu = jnp.zeros((high, wide), jnp.float32)
+            for k in range(K):
+                glu = glu + taps[pl.ds(k, 1), :] * back[pl.ds(start + (edge + HALF - k), high), :]
+            sig = sigmoid(gate[rows, :])
+            v_grad[rows, :] = (glu * sig).astype(jnp.bfloat16)
+            g_grad[rows, :] = (glu * value[rows, :] * sig * (1.0 - sig)).astype(jnp.bfloat16)
+            own = back[pl.ds(pl.multiple_of(edge + i * high, edge), high), :]
+
+            def eights(block):
+                part = block[:8]
+                for j in range(1, high // 8):
+                    part = part + block[8 * j : 8 * j + 8]
+                return part
+
+            for k in range(K):
+                term = own * ahead[pl.ds(start + (edge - HALF + k), high), :]
+                tap_grads[k] = tap_grads[k] + eights(term)
+            tap_grads[K] = tap_grads[K] + eights(own)
+
+
+def conv_stage(value_pre, gate_pre, act_grad, taps, bias):
+    total, own = value_pre.shape
+    bounds = clips(total)
+    longest = max(end - begin for begin, end in bounds)
+    half = jax.ShapeDtypeStruct((total, own), jnp.bfloat16)
+    return pl.pallas_call(
+        lambda *refs: conv_body(bounds, *refs),
+        out_shape=[half, half, half, jax.ShapeDtypeStruct((K + 1, 8, own), jnp.float32)],
+        in_specs=[VMEM] * 5,
+        out_specs=[VMEM] * 4,
+        scratch_shapes=[pltpu.VMEM((longest + 32, own), jnp.float32)] * 2,
+        compiler_params=pltpu.CompilerParams(vmem_limit_bytes=32 * 2**20),
+        cost_estimate=pl.CostEstimate(flops=6 * K * total * own, bytes_accessed=4_000_000, transcendentals=0),
+    )(value_pre, gate_pre, act_grad, taps, bias)
 
 
 def shards(frames, gain, w_value, w_gate, kernel, bias, w_out, grad_out):
@@ -666,40 +737,10 @@
         (value_part, gate_part, act_part, eight(scaled)),
     )
     scaled = lax.dynamic_slice_in_dim(jnp.sum(scaled, axis=0), r * own, own, 1)
-    gate_sig = jax.nn.sigmoid(gate_pre)
-    gated = (value_pre * gate_sig).astype(jnp.bfloat16).astype(jnp.float32)
-    taps = lax.dynamic_slice_in_dim(kernel, r * own, own, 1)
-    own_bias = lax.dynamic_slice_in_dim(bias, r * own, own, 0)
-    conv_parts, glu_parts = [], []
-    for begin, end in clips(total):
-        ahead = padded(gated[begin:end])
-        conv = jnp.zeros((end - begin, own), jnp.float32) + own_bias[None, :]
-        for k in range(K):
-            conv = conv + taps[k][None, :] * ahead[k : k + end - begin]
-        conv_parts.append(conv)
-    conv_pre = jnp.concatenate(conv_parts, axis=0)
-    conv_sig = jax.nn.sigmoid(conv_pre)
-    activated = (conv_pre * conv_sig).astype(jnp.bfloat16)
-    conv_grad = (
-        act_grad.astype(jnp.float32) * conv_sig * (1.0 + conv_pre * (1.0 - conv_sig))
-    ).astype(jnp.bfloat16)
-    conv_wide = conv_grad.astype(jnp.float32)
-    tap_grads = jnp.zeros((K, own), jnp.float32)
-    for begin, end in clips(total):
-        back = padded(conv_wide[begin:end])
-        ahead = padded(gated[begin:end])
-        glu = jnp.zeros((end - begin, own), jnp.float32)
-        tap_rows = []
-        for k in range(K):
-            glu = glu + taps[k][None, :] * back[2 * HALF - k : 2 * HALF - k + end - begin]
-            tap_rows.append(jnp.sum(conv_wide[begin:end] * ahead[k : k + end - begin], axis=0))
-        glu_parts.append(glu)
-        tap_grads = tap_grads + jnp.stack(tap_rows)
-    glu_grad = jnp.concatenate(glu_parts, axis=0)
-    value_grad = (glu_grad * gate_sig).astype(jnp.bfloat16)
-    gate_grad = (glu_grad * value_pre * gate_sig * (1.0 - gate_sig)).astype(jnp.bfloat16)
-    bias_grad = jnp.sum(conv_wide, axis=0)
-    depthwise = jnp.concatenate([tap_grads, bias_grad[None, :]], axis=0)
+    taps = jnp.pad(lax.dynamic_slice_in_dim(kernel, r * own, own, 1), ((0, 1), (0, 0)))
+    own_bias = eight(lax.dynamic_slice_in_dim(bias, r * own, own, 0)[None, :])
+    activated, value_grad, gate_grad, tap_grads = conv_stage(value_pre, gate_pre, act_grad, taps, own_bias)
+    depthwise = jnp.sum(tap_grads, axis=1)
     value_wide, gate_wide = value_grad.astype(jnp.float32), gate_grad.astype(jnp.float32)
     norm_sums = jnp.stack(
         [

time: 307 us -> 299 us (0.974)
  other arithmetic: 28.5 us -> 10.6 us
  Pallas kernels: 230 us -> 238 us
    reduce_sum x2 -> x1, other arithmetic: 9.53 us -> 0.94 us  [shards(): depthwise = jnp.sum(tap_grads, axis=1)]
    pallas_call x0 -> x1, Pallas kernels: none -> 7.67 us  [conv_stage(): pl.pallas_call(lambda *refs: conv_body(bounds, *refs), out_shape=[half, h...]
    unnamed x79 -> x69, local copies, waits for them, and re-layouts: 12.5 us -> 20 us
    reduce_sum x1, other arithmetic: 5.19 us -> 0.6 us  [shards(): jnp.sum(value_wide * scaled[0][None, :] + gate_wide * scaled[1][None, :],...]
    convert_element_type x3 -> x0, other arithmetic: 3.98 us -> none  [the longest x1 1.59 us: shards(): gated = (value_pre * gate_sig).astype(jnp.bfloat16).astype(jnp.float32)]
    mul x2 -> x1, local copies, waits for them, and re-layouts: 3.24 us -> 0.01 us  [shards(): value_wide * scaled[0][None, :] + gate_wide * scaled[1][None, :]]
where the time goes in v1:
time: 299 us
  Pallas kernels  238 us (80%)
  local copies, waits for them, and re-layouts  27 us (9%)
  matrix products  21.7 us (7%)
  other arithmetic  10.6 us (4%)
    pallas_call x4, Pallas kernels, exchange(): pl.pallas_call(body, out_shape=out_shape, in_specs=in_specs, out_specs=ou...  231 us
    dot_general x8, matrix products, dot(): lax.dot_general(left, right, ((contract[:1], contract[1:]), ((), ())), pr...  21.7 us
    unnamed x69, local copies, waits for them, and re-layouts  20 us
    pallas_call x1, Pallas kernels, conv_stage(): pl.pallas_call(lambda *refs: conv_body(bounds, *refs), out_shape=[half, h...  7.67 us

profile of v1, /device:TPU:0, one launch (start us, length us, event | category | flops | bytes accessed | tf_op | source)
XLA Modules:
  0.0 298.6 jit_solution(2773429308740312806)
XLA Ops:
  2.1 1.2 convert_reduce_fusion
  4.1 1.5 convolution_reduce_fusion.1
  5.6 1.5 convolution_reduce_fusion
  7.8 1.0 copy-done.3
  8.8 1.0 copy-done.13
  9.8 46.9 %shard_map.143 = (bf16[1536,1024]{1,0:T(8,128)(2,1)}, bf16[1536,512]{1,0:T(8,128)(2,1)S(1)}, f32[4,8,384]{2,1,0:T(8,128)S(1)}) custom-call(bf16[384,512]{1,0:T(8,128)(2,1)S(1)} %copy-done.3, bf16[384,512]{1,0:T(8,128)(2,1)S(1)} %copy-done.13, f32[8,384]{1,0:T(8,128)S(1)} %select_maximum_fusion.2.refs_2_), custom_call_target="tpu_custom_call" | custom-call | bytes 100000000 | tf_op jit(solution)/shard_map/pallas_call | solution.py:587
  56.7 1.1 copy-done.9
  58.6 2.6 multiply_convert_fusion.refs_2_
  61.9 3.0 convolution_convert_fusion.2.refs_1_
  64.9 1.8 convolution_convert_fusion.3.refs_0_
  66.8 3.5 %convolution_convert_fusion.refs_2_ = bf16[1536,1024]{1,0:T(8,128)(2,1)} fusion(bf16[1536,512]{1,0:T(8,128)(2,1)S(1)} %copy-done.10, bf16[1024,512]{1,0:T(8,128)(2,1)S(1)} %copy-done), kind=kOutput, calls=%fused_computation.2 | convolution fusion | flops 1612185600 | bytes 5767168 | tf_op jit(solution)/shard_map/dot_general | solution.py:601
  70.3 62.6 %shard_map.144 = (f32[1536,128]{1,0:T(8,128)S(1)}, f32[1536,128]{1,0:T(8,128)S(1)}, bf16[1536,128]{1,0:T(8,128)(2,1)S(1)}, f32[4,8,512]{2,1,0:T(8,128)S(1)}) custom-call(bf16[1536,512]{1,0:T(8,128)(2,1)S(1)} %convolution_convert_fusion.3.refs_0_, bf16[1536,512]{1,0:T(8,128)(2,1)} %convolution_convert_fusion.2.refs_1_, ...), custom_call_target="tpu_custom_call" | custom-call | bytes 100000000 | tf_op jit(solution)/shard_map/pallas_call | solution.py:587
  135.5 1.1 copy-done.6
  136.6 1.1 copy-done.8
  137.7 1.0 copy-done.20
  139.4 7.7 %shard_map.145 = (bf16[1536,128]{1,0:T(8,128)(2,1)S(1)}, bf16[1536,128]{1,0:T(8,128)(2,1)S(1)}, bf16[1536,128]{1,0:T(8,128)(2,1)S(1)}, f32[32,8,128]{2,1,0:T(8,128)S(1)}) custom-call(f32[1536,128]{1,0:T(8,128)S(1)} %copy-done.6, f32[1536,128]{1,0:T(8,128)S(1)} %copy-done.8, bf16[1536,128]{1,0:T(8,128)(2,1)S(1)} %copy-done.20, f32[32,128]{1,0:T(8,128)S(1)} %pad.27.refs_3_, ...), custom_call_target="tpu_custom_call" | custom-call | flops 36569088 | bytes 4000000 | tf_op jit(solution)/shard_map/pallas_call | solution.py:676
  150.9 1.0 copy-done.16
  151.9 1.0 copy-done.18
  152.9 47.4 %shard_map.146 = (bf16[1536,1024]{1,0:T(8,128)(2,1)}, bf16[1536,512]{1,0:T(8,128)(2,1)S(1)}, bf16[1536,512]{1,0:T(8,128)(2,1)}, f32[4,8,1536]{2,1,0:T(8,128)S(1)}, f32[4,32,128]{2,1,0:T(8,128)S(1)}) custom-call(bf16[1536,128]{1,0:T(8,128)(2,1)S(1)} %copy-done.18, bf16[1536,128]{1,0:T(8,128)(2,1)S(1)} %get-tuple-element.37.refs_1_, ...), custom_call_target="tpu_custom_call" | custom-call | bytes 100000000 | tf_op jit(solution)/shard_map/pallas_call | solution.py:587
  200.3 1.1 copy-done.11
  202.7 0.9 reduce_sum.89
  203.7 1.3 slice.45
  206.6 5.0 %convolution_convert_fusion.1.refs_0_ = bf16[1536,512]{1,0:T(8,128)(2,1)} fusion(bf16[1536,1024]{1,0:T(8,128)(2,1)} %get-tuple-element.41.refs_3_, bf16[1024,512]{1,0:T(8,128)(2,1)S(1)} %copy-done), kind=kOutput, calls=%fused_computation.3 | convolution fusion | flops 1611399168 | bytes 5767168 | tf_op jit(solution)/shard_map/dot_general | solution.py:601
  211.5 1.9 fusion.21
  213.4 3.6 %add_convert_fusion.refs_1_ = bf16[1536,1024]{1,0:T(8,128)(2,1)} fusion(f32[1536,1024]{1,0:T(8,128)S(1)} %fusion.21, bf16[1536,512]{1,0:T(8,128)(2,1)S(1)} %copy-done.26, bf16[1024,512]{1,0:T(8,128)(2,1)S(1)} %copy-done.1), kind=kOutput, calls=%fused_computation | convolution fusion | flops 1613758464 | bytes 12058624 | tf_op jit(solution)/shard_map/dot_general | solution.py:601
  217.1 73.7 %shard_map.147 = (f32[384,512]{1,0:T(8,128)S(1)}, bf16[384,512]{1,0:T(8,128)(2,1)S(1)}, f32[1024,512]{1,0:T(8,128)}, f32[1024,512]{1,0:T(8,128)}, f32[1024,512]{1,0:T(8,128)}, /*index=5*/f32[4,8,128]{2,1,0:T(8,128)S(1)}) custom-call(bf16[1536,512]{1,0:T(8,128)(2,1)} %convolution_convert_fusion.1.refs_0_, bf16[1536,1024]{1,0:T(8,128)(2,1)} %add_convert_fusion.refs_1_, ...), custom_call_target="tpu_custom_call" | custom-call | bytes 100000000 | tf_op jit(solution)/shard_map/pallas_call | solution.py:587
  290.8 1.5 dynamic-slice_divide_fusion
  292.3 1.2 fusion.11
  293.6 1.3 copy.21
  294.9 1.3 copy.22
  296.2 1.0 copy-done.27
  297.2 1.3 copy.23
  (87 shorter events, 14.3 us)
Async XLA Ops:
  0.6 66.1 %copy-start = (bf16[1024,512]{1,0:T(8,128)(2,1)S(1)}, bf16[1024,512]{1,0:T(8,128)(2,1)}, u32[]{:S(2)}) copy-start(bf16[1024,512]{1,0:T(8,128)(2,1)} %param.14) | copy-start | bytes 3145732
  7.8 1.0 copy-start.3
  8.8 1.0 copy-start.13
  56.7 1.1 copy-start.9
  58.5 3.4 %copy-start.1 = (bf16[1024,512]{1,0:T(8,128)(2,1)S(1)}, bf16[1024,512]{1,0:T(8,128)(2,1)}, u32[]{:S(2)}) copy-start(bf16[1024,512]{1,0:T(8,128)(2,1)} %refs_8_.1) | copy-start | bytes 3145732
  61.2 3.7 %copy-start.25 = (bf16[1536,1024]{1,0:T(8,128)(2,1)}, bf16[1536,1024]{1,0:T(8,128)(2,1)S(1)}, u32[]{:S(2)}) copy-start(bf16[1536,1024]{1,0:T(8,128)(2,1)S(1)} %multiply_convert_fusion.refs_2_) | copy-start | bytes 9437188
  61.9 3.0 copy-start.2
  64.9 1.9 copy-start.10
  132.9 0.9 copy-start.5
  133.8 0.9 copy-start.7
  134.7 0.7 copy-start.19
  135.4 1.1 copy-start.6
  136.6 1.1 copy-start.8
  137.7 1.0 copy-start.20
  138.7 0.7 copy-start.24
  147.1 0.7 copy-start.15
  147.1 0.9 copy-start.17
  147.1 0.9 copy-start.22
  150.9 1.0 copy-start.16
  151.9 1.0 copy-start.18
  200.3 1.1 copy-start.11
  201.4 0.7 copy-start.21
  202.1 0.6 copy-start.23
  206.6 5.0 %copy-start.12 = (bf16[1536,512]{1,0:T(8,128)(2,1)S(1)}, bf16[1536,512]{1,0:T(8,128)(2,1)}, u32[]{:S(2)}) copy-start(bf16[1536,512]{1,0:T(8,128)(2,1)} %copy-done.11) | copy-start | bytes 4718596
  211.5 1.9 copy-start.26
  217.0 75.3 %copy-start.4 = (bf16[384,512]{1,0:T(8,128)(2,1)S(1)}, bf16[384,512]{1,0:T(8,128)(2,1)}, u32[]{:S(2)}) copy-start(bf16[384,512]{1,0:T(8,128)(2,1)} %refs_0_.1) | copy-start | bytes 1179652
  217.0 75.3 %copy-start.14 = (bf16[384,512]{1,0:T(8,128)(2,1)S(1)}, bf16[384,512]{1,0:T(8,128)(2,1)}, u32[]{:S(2)}) copy-start(bf16[384,512]{1,0:T(8,128)(2,1)} %refs_1_.1) | copy-start | bytes 1179652
  217.0 75.3 %copy-start.30 = (f32[384]{0:T(512)S(1)}, f32[384]{0:T(512)}, u32[]{:S(2)}) copy-start(f32[384]{0:T(512)} %dynamic_slice.34) | copy-start | bytes 4612
  217.0 75.3 %copy-start.31 = (f32[384]{0:T(512)S(1)}, f32[384]{0:T(512)}, u32[]{:S(2)}) copy-start(f32[384]{0:T(512)} %dynamic_slice.31) | copy-start | bytes 4612
  290.8 2.8 copy-start.29
  292.3 2.6 copy-start.28
  294.9 2.3 copy-start.27
